TPU v7x, 32 devices: a whole 2x2x4 slice. The times are simulated.
32 devices in a mesh: group: 2 (over x), fsdp: 8 (over z, y), tp: 2 (over core).
Axes of the slice: x: 2, y: 2, z: 4, core: 2. Of those that a mesh axis runs over, the one named last changes fastest.
Arguments:
- tokens: bfloat16 [16384, 8192], P(('group', 'fsdp'), 'tp'), parts along dimension 0, may hold values from -6 to 6
- cotangent: bfloat16 [16384, 1024], P(('group', 'fsdp'), 'tp'), parts along dimension 0, may hold values from -0.059814453 to 0.059814453
- frozen_rows: bfloat16 [1024, 8192], P('fsdp', 'tp'), may hold values from -0.0625 to 0.0625
- rank_down: bfloat16 [1024, 8192], P(('group', 'fsdp'), 'tp'), parts along dimension 0, may hold values from -0.0625 to 0.0625
- rank_up: bfloat16 [1024, 1024], P(('group', 'fsdp'), 'tp'), parts along dimension 0, may hold values from -1.5 to 1.5
- counts: int32 [16], P(('group', 'fsdp')), parts along dimension 0, may hold values from 1 to 2, as said below
- tenants: int32 [32], P(('group', 'fsdp')), parts along dimension 0, may hold values from 0 to 31
Outputs:
- projected: bfloat16 [16384, 1024], P(('group', 'fsdp'), 'tp'), parts along dimension 0
- grad_down: float32 [1024, 8192], P(('group', 'fsdp'), 'tp'), parts along dimension 0
- grad_up: float32 [1024, 1024], P(('group', 'fsdp'), 'tp'), parts along dimension 0
There are 2 independent parts, one for each index of `group`. A program takes and returns all parts, laid end to end along the dimension named above; an argument that names none is the same for every part. Nothing has to cross between parts.
Inputs may be any that keep to these rules, and one draw needn't show every extreme that they name: Device f holds counts[f] live blocks in its first slots; in every draw some device has all 2 slots live.
All inputs are finite; a program needn't handle non-finite values.
Results may differ from a plain program's by a relative error of at most 0.0045.
Values may be sent and summed in bfloat16 or wider, within the bound.
A program may use at most 128 MiB of HBM per device.

v0:
```python
import jax
import jax.numpy as jnp
from jax import lax
from jax.sharding import PartitionSpec as P

RANK = 16
BLOCK = 512
SLOTS = 2


adapter_scale = 2.0


def partial_stacks(token_blocks, cot_blocks, tenant_ids, live_count, weights):
    frozen_all, down_all, up_all = weights
    number = token_blocks.shape[0]
    contract = (((1,), (1,)), ((), ()))
    start = (
        jnp.zeros((number, BLOCK, frozen_all.shape[0]), jnp.float32),
        jnp.zeros((number, BLOCK, RANK), jnp.float32),
        jnp.zeros((number, BLOCK, RANK), jnp.float32),
    )

    def partial_loop_body(index, carried):
        frozen_stack, low_stack, back_stack = carried
        row_block = lax.dynamic_index_in_dim(token_blocks, index, 0, keepdims=False)
        cot_block = lax.dynamic_index_in_dim(cot_blocks, index, 0, keepdims=False)
        tenant = lax.dynamic_index_in_dim(tenant_ids, index, 0, keepdims=False)
        offset = tenant * RANK
        down_rows = lax.dynamic_slice_in_dim(down_all, offset, RANK, 0)
        up_weight_rows = lax.dynamic_slice_in_dim(up_all, offset, RANK, 0)
        partial_frozen = lax.dot_general(
            row_block, frozen_all, contract, preferred_element_type=jnp.float32
        )
        low_part = lax.dot_general(
            row_block, down_rows, contract, preferred_element_type=jnp.float32
        )
        back_part = lax.dot_general(
            cot_block, up_weight_rows, contract, preferred_element_type=jnp.float32
        )
        frozen_stack = lax.dynamic_update_index_in_dim(frozen_stack, partial_frozen, index, 0)
        low_stack = lax.dynamic_update_index_in_dim(low_stack, low_part, index, 0)
        back_stack = lax.dynamic_update_index_in_dim(back_stack, back_part, index, 0)
        return (frozen_stack, low_stack, back_stack)

    return lax.fori_loop(0, live_count, partial_loop_body, start)


def add_terms(grad_total, term, offset):
    current = lax.dynamic_slice_in_dim(grad_total, offset, RANK, 0)
    return lax.dynamic_update_slice_in_dim(grad_total, current + term, offset, 0)


def keep_dense(store, index, down_projection_term, up_projection_term, offset):
    return (
        add_terms(store[0], down_projection_term, offset),
        add_terms(store[1], up_projection_term, offset),
    )


def run_blocks(token_blocks, cot_blocks, tenant_ids, live_count, results, store, weights, keep):
    frozen_stack, low_stack, back_stack = partial_stacks(
        token_blocks, cot_blocks, tenant_ids, live_count, weights
    )
    low_summed, back_summed = lax.psum((low_stack, back_stack), "tp")
    frozen_summed = lax.psum_scatter(frozen_stack, "tp", scatter_dimension=2, tiled=True)
    up_all = weights[2]
    columns = (((0,), (0,)), ((), ()))

    def run_loop_body(index, carried):
        results_now, store_now = carried
        row_block = lax.dynamic_index_in_dim(token_blocks, index, 0, keepdims=False)
        cot_block = lax.dynamic_index_in_dim(cot_blocks, index, 0, keepdims=False)
        tenant = lax.dynamic_index_in_dim(tenant_ids, index, 0, keepdims=False)
        offset = tenant * RANK
        up_weight_rows = lax.dynamic_slice_in_dim(up_all, offset, RANK, 0)
        lower_half = lax.dynamic_index_in_dim(low_summed, index, 0, keepdims=False).astype(
            jnp.bfloat16
        )
        back_half = lax.dynamic_index_in_dim(back_summed, index, 0, keepdims=False).astype(
            jnp.bfloat16
        )
        frozen_output = lax.dynamic_index_in_dim(frozen_summed, index, 0, keepdims=False)
        final_result = (
            frozen_output
            + adapter_scale
            * jnp.dot(lower_half, up_weight_rows, preferred_element_type=jnp.float32)
        ).astype(jnp.bfloat16)
        down_projection_term = adapter_scale * lax.dot_general(
            back_half, row_block, columns, preferred_element_type=jnp.float32
        )
        up_projection_term = adapter_scale * lax.dot_general(
            lower_half, cot_block, columns, preferred_element_type=jnp.float32
        )
        results_now = lax.dynamic_update_index_in_dim(results_now, final_result, index, 0)
        store_now = keep(store_now, index, down_projection_term, up_projection_term, offset)
        return (results_now, store_now)

    return lax.fori_loop(0, live_count, run_loop_body, (results, store))


def local(tokens, cotangent, frozen_rows, rank_down, rank_up, counts, tenants):
    weights = (
        lax.all_gather(frozen_rows, "fsdp", axis=0, tiled=True),
        lax.all_gather(rank_down, "fsdp", axis=0, tiled=True),
        lax.all_gather(rank_up, "fsdp", axis=0, tiled=True),
    )
    half_d = tokens.shape[1]
    half_v = cotangent.shape[1]
    token_blocks = tokens.reshape(SLOTS, BLOCK, half_d)
    cot_blocks = cotangent.reshape(SLOTS, BLOCK, half_v)
    results = jnp.zeros((SLOTS, BLOCK, half_v), jnp.bfloat16)
    total_rows = weights[1].shape[0]
    own_store = (
        jnp.zeros((total_rows, half_d), jnp.float32),
        jnp.zeros((total_rows, half_v), jnp.float32),
    )
    own_count = counts[0]
    results, final_store = run_blocks(
        token_blocks, cot_blocks, tenants, own_count, results, own_store, weights, keep_dense
    )
    grad_down, grad_up = (
        lax.psum_scatter(final_store[0], "fsdp", scatter_dimension=0, tiled=True),
        lax.psum_scatter(final_store[1], "fsdp", scatter_dimension=0, tiled=True),
    )
    return (results.reshape(SLOTS * BLOCK, half_v), grad_down, grad_up)


def solution(mesh):
    in_specs = (
        P(("group", "fsdp"), "tp"),
        P(("group", "fsdp"), "tp"),
        P("fsdp", "tp"),
        P(("group", "fsdp"), "tp"),
        P(("group", "fsdp"), "tp"),
        P(("group", "fsdp")),
        P(("group", "fsdp")),
    )
    out_specs = (P(("group", "fsdp"), "tp"), P(("group", "fsdp"), "tp"), P(("group", "fsdp"), "tp"))
    return jax.shard_map(local, mesh=mesh, in_specs=in_specs, out_specs=out_specs, check_vma=False)
```

profile of v0, /device:TPU:0, one launch (start us, length us, event | category | flops | bytes accessed | tf_op | source)
XLA Modules:
  0.0 508.6 jit_solution(5088623312577953317)
XLA Ops:
  8.0 0.7 all-gather.3.cloned.1.call-update
  8.7 34.8 %all_gather.11 = bf16[512,512]{1,0:T(8,128)(2,1)S(1)} all-gather(bf16[64,512]{1,0:T(8,128)(2,1)} %param.15), channel_id=1, replica_groups=mesh['group'=2,'fsdp'=8,'tp'=2] {'fsdp'}, dimensions={0}, use_global_device_ids=true | all-gather | bytes 589824 | tf_op jit(solution)/shard_map/all_gather | solution.py:106
  43.5 45.5 %all-gather.5.cloned.1.call-done = bf16[512,4096]{1,0:T(8,128)(2,1)} async-done(((bf16[64,4096]{1,0:T(8,128)(2,1)}), bf16[512,4096]{1,0:T(8,128)(2,1)}) %all-gather.5.cloned.1.call-update) | async-done | bytes 4194320 | tf_op jit(solution)/shard_map/all_gather | solution.py:105
  89.1 125.4 %all-gather.3.cloned.1.call-done = bf16[1024,4096]{1,0:T(8,128)(2,1)} async-done(((bf16[128,4096]{1,0:T(8,128)(2,1)}), bf16[1024,4096]{1,0:T(8,128)(2,1)}) %all-gather.3.cloned.1.call-update) | async-done | bytes 8388624 | tf_op jit(solution)/shard_map/all_gather | solution.py:104
  214.4 2.5 broadcast_in_dim.30
  216.9 32.7 %while.28 = (s32[]{:T(128)}, f32[2,512,1024]{2,1,0:T(8,128)}, f32[2,512,16]{1,2,0:T(8,128)S(1)}, f32[2,512,16]{1,2,0:T(8,128)S(1)}, s32[]{:T(128)}, /*index=5*/b...) while((s32[]{:T(128)}, f32[2,512,1024]{2,1,0:T(8,128)}, ...), condition=%wide.region_1.2_spmd, body=%wide.region_0.1_spmd.sunk | while | flops 4370464768 | bytes 19615984 | solution.py:46
  218.8 3.4 fusion.67
  222.5 10.5 %bitcast_dynamic-update-slice_fusion.2 = f32[2,512,1024]{2,1,0:T(8,128)} fusion(f32[2,512,1024]{2,1,0:T(8,128)} %get-tuple-element.341, s32[]{:T(128)S(6)} %select_n.40, bf16[1024,4096]{1,0:T(8,128)(2,1)} %get-tuple-element.362, bf16[2,512,4096]{2,1,0:T(8,128)(2,1)} %get-tuple-element.361), kind=kOutput, calls=%fused_computation.6.clone.1 | convolution fusion | flops 4294967296 | bytes 14681088 | tf_op jit(solution)/shard_map/while/body/dot_general | solution.py:32
  234.9 3.4 fusion.67
  238.5 10.5 %bitcast_dynamic-update-slice_fusion.2 = f32[2,512,1024]{2,1,0:T(8,128)} fusion(f32[2,512,1024]{2,1,0:T(8,128)} %get-tuple-element.341, s32[]{:T(128)S(6)} %select_n.40, bf16[1024,4096]{1,0:T(8,128)(2,1)} %get-tuple-element.362, bf16[2,512,4096]{2,1,0:T(8,128)(2,1)} %get-tuple-element.361), kind=kOutput, calls=%fused_computation.6.clone.1 | convolution fusion | flops 4294967296 | bytes 14681088 | tf_op jit(solution)/shard_map/while/body/dot_general | solution.py:32
  249.8 3.9 all-reduce.2
  253.6 6.5 %reduce-scatter.4.cloned.1.call-done = f32[2,512,512]{2,1,0:T(8,128)} async-done(((f32[2,512,1024]{2,1,0:T(8,128)}), f32[2,512,512]{2,1,0:T(8,128)}) %reduce-scatter.4.cloned.1.call-update) | async-done | bytes 2097168 | tf_op jit(solution)/shard_map/reduce_scatter | solution.py:66
  260.1 4.3 broadcast_in_dim.28
  264.4 1.0 broadcast_in_dim.27
  265.4 1.1 broadcast_in_dim.29
  266.5 18.5 %while.29 = (s32[]{:T(128)}, bf16[2,512,512]{2,1,0:T(8,128)(2,1)}, f32[512,4096]{1,0:T(8,128)}, f32[512,512]{1,0:T(8,128)}, s32[]{:T(128)}, /*index=5*/f32[2,512...) while((s32[]{:T(128)}, bf16[2,512,512]{2,1,0:T(8,128)(2,1)}, ...), condition=%wide.region_6.7_spmd, body=%wide.region_5.6_spmd.sunk | while | flops 84819976 | bytes 6951673 | solution.py:99
  268.5 3.6 fusion.76
  272.1 1.6 fusion.77
  273.6 1.8 fusion.75
  277.4 3.6 fusion.76
  281.0 1.6 fusion.77
  282.5 1.8 fusion.75
  285.6 64.4 %reduce-scatter.8.cloned.1.call-done = f32[64,512]{1,0:T(8,128)} async-done(((f32[512,512]{1,0:T(8,128)}), f32[64,512]{1,0:T(8,128)}) %reduce-scatter.8.cloned.1.call-update) | async-done | bytes 131088 | tf_op jit(solution)/shard_map/reduce_scatter | solution.py:124
  350.0 152.1 %reduce-scatter.6.cloned.1.call-done = f32[64,4096]{1,0:T(8,128)} async-done(((f32[512,4096]{1,0:T(8,128)}), f32[64,4096]{1,0:T(8,128)}) %reduce-scatter.6.cloned.1.call-update) | async-done | bytes 1048592 | tf_op jit(solution)/shard_map/reduce_scatter | solution.py:123
  (25 shorter events, 4.4 us)
Async XLA Ops:
  7.2 209.7 %copy-start = (bf16[1024,512]{1,0:T(8,128)(2,1)S(1)}, bf16[1024,512]{1,0:T(8,128)(2,1)}, u32[]{:S(2)}) copy-start(bf16[1024,512]{1,0:T(8,128)(2,1)} %param.12) | copy-start | bytes 3145732
  7.2 209.7 %copy-start.3 = (s32[2]{0:T(128)S(1)}, s32[2]{0:T(128)}, u32[]{:S(2)}) copy-start(s32[2]{0:T(128)} %param.17) | copy-start | bytes 28
  7.2 81.9 %all-gather.5.cloned.1.call-start = ((), (), s32[]{:S(2)}) async-start(), calls=%async_computation.4 | async-start | bytes 4718592 | tf_op jit(solution)/shard_map/all_gather | solution.py:105
  7.9 206.5 %all-gather.3.cloned.1.call-start = ((), (), s32[]{:S(2)}) async-start(), calls=%async_computation.3 | async-start | bytes 9437184 | tf_op jit(solution)/shard_map/all_gather | solution.py:104
  8.7 251.5 %reduce-scatter.4.cloned.1.call-start = ((), (), s32[]{:S(2)}) async-start(), calls=%async_computation.5 | async-start | bytes 6291456 | tf_op jit(solution)/shard_map/reduce_scatter | solution.py:66
  249.7 10.4 %copy-start.2 = (bf16[512,512]{1,0:T(8,128)(2,1)}, bf16[512,512]{1,0:T(8,128)(2,1)S(1)}, u32[]{:S(2)}) copy-start(bf16[512,512]{1,0:T(8,128)(2,1)S(1)} %get-tuple-element.435) | copy-start | bytes 1572868
  249.7 100.3 %reduce-scatter.8.cloned.1.call-start = ((), (), s32[]{:S(2)}) async-start(), calls=%async_computation.7 | async-start | bytes 1179648 | tf_op jit(solution)/shard_map/reduce_scatter | solution.py:124
  260.1 6.4 %copy-start.1 = (f32[2,512,512]{2,1,0:T(8,128)S(1)}, f32[2,512,512]{2,1,0:T(8,128)}, u32[]{:S(2)}) copy-start(f32[2,512,512]{2,1,0:T(8,128)} %reduce-scatter.4.cloned.1.call-done) | copy-start | bytes 6291460
  285.1 217.0 %reduce-scatter.6.cloned.1.call-start = ((), (), s32[]{:S(2)}) async-start(), calls=%async_computation.6 | async-start | bytes 9437184 | tf_op jit(solution)/shard_map/reduce_scatter | solution.py:123
Sparse Core Ops, SparseCore 0:
  10.1 78.8 all-gather.4
  91.2 123.1 all-gather.2
  249.8 10.2 reduce-scatter.3
  285.2 64.7 reduce-scatter.7
  354.0 147.9 reduce-scatter.5
where the time goes:
time: 509 us
  waiting for transfers between devices  396 us (78%)
  matrix products  42.2 us (8%)
  blocking collectives  38.7 us (8%)
  between operations  13.8 us (3%)
  local copies, waits for them, and re-layouts  11.3 us (2%)
  loops' own time  6.54 us (1%)
    reduce_scatter x1, waiting for transfers between devices, local(): lax.psum_scatter(final_store[0], 'fsdp', scatter_dimension=0, tiled=True)  152 us
    all_gather x1, waiting for transfers between devices, local(): lax.all_gather(frozen_rows, 'fsdp', axis=0, tiled=True)  125 us
    reduce_scatter x1, waiting for transfers between devices, local(): lax.psum_scatter(final_store[1], 'fsdp', scatter_dimension=0, tiled=True)  64.4 us
    all_gather x1, waiting for transfers between devices, local(): lax.all_gather(rank_down, 'fsdp', axis=0, tiled=True)  45.5 us
    all_gather x1, blocking collectives, local(): lax.all_gather(rank_up, 'fsdp', axis=0, tiled=True)  34.8 us
    dot_general x2, matrix products, partial_loop_body(): lax.dot_general(row_block, frozen_all, contract, preferred_element_type=j...  21 us
  transfers between devices with their start and end apart: 5, of which 5 were waited for; matrix products, arithmetic and copies ran while one was open for 0% of the time, Pallas kernels for 0%

commit v1 on v0

v1 whole, which is shorter than its diff:
```python
import jax
import jax.numpy as jnp
from jax import lax
from jax.sharding import PartitionSpec as P

RANK = 16
BLOCK = 512
SLOTS = 2
SCALE = 2.0

CONTRACT = (((1,), (1,)), ((), ()))
COLUMNS = (((0,), (0,)), ((), ()))


def gather(x):
    return lax.all_gather(x, "fsdp", axis=0, tiled=True)


def rows_of(table, tenants):
    return [
        lax.dynamic_slice_in_dim(table, tenants[s] * RANK, RANK, 0) for s in range(SLOTS)
    ]


def owner_sum(terms, chosen):
    return jnp.dot(chosen, terms, preferred_element_type=jnp.float32)


def swap_cores(x):
    return lax.ppermute(x, "tp", [(0, 1), (1, 0)])


def sum_cores(x):
    return x + swap_cores(x)


def local(tokens, cotangent, frozen_rows, rank_down, rank_up, counts, tenants):
    me = lax.axis_index("fsdp")
    owned = rank_down.shape[0]
    live = jnp.arange(SLOTS, dtype=jnp.int32) < counts[0]
    live_f = jnp.where(live, SCALE, 0.0).astype(jnp.float32)
    x = [tokens[s * BLOCK : (s + 1) * BLOCK] for s in range(SLOTS)]
    g = [cotangent[s * BLOCK : (s + 1) * BLOCK] for s in range(SLOTS)]

    up_all = gather(rank_up)
    ids_all = gather(jnp.where(live, tenants, -1))
    mine = me * owned + jnp.arange(owned, dtype=jnp.int32)
    sent = (ids_all[:, None] * RANK + jnp.arange(RANK, dtype=jnp.int32)).reshape(-1)
    chosen = (mine[:, None] == sent[None, :]).astype(jnp.bfloat16)

    up = rows_of(up_all, tenants)
    back_part = jnp.stack(
        [lax.dot_general(g[s], up[s], CONTRACT, preferred_element_type=jnp.float32) for s in range(SLOTS)]
    )
    back = sum_cores(back_part).astype(jnp.bfloat16)
    down_terms = jnp.concatenate(
        [
            (live_f[s] * lax.dot_general(back[s], x[s], COLUMNS, preferred_element_type=jnp.float32))
            for s in range(SLOTS)
        ]
    ).astype(jnp.bfloat16)
    down_all = gather(rank_down)
    down_terms_all = gather(down_terms)
    frozen_all = gather(frozen_rows)

    down = rows_of(down_all, tenants)
    low_part = jnp.stack(
        [lax.dot_general(x[s], down[s], CONTRACT, preferred_element_type=jnp.float32) for s in range(SLOTS)]
    )
    low = sum_cores(low_part).astype(jnp.bfloat16)
    up_terms = jnp.concatenate(
        [
            (live_f[s] * lax.dot_general(low[s], g[s], COLUMNS, preferred_element_type=jnp.float32))
            for s in range(SLOTS)
        ]
    ).astype(jnp.bfloat16)
    up_terms_all = gather(up_terms)
    grad_down = owner_sum(down_terms_all, chosen)
    grad_up = owner_sum(up_terms_all, chosen)

    half = cotangent.shape[1]
    core = lax.axis_index("tp")

    def frozen_half(which):
        weight = lax.dynamic_slice_in_dim(frozen_all, which * half, half, 0)
        return lax.dot_general(tokens, weight, CONTRACT, preferred_element_type=jnp.float32)

    received = swap_cores(frozen_half(1 - core))
    frozen = frozen_half(core) + received
    adapted = jnp.concatenate(
        [
            SCALE * jnp.dot(low[s], up[s], preferred_element_type=jnp.float32)
            for s in range(SLOTS)
        ]
    )
    keep = jnp.repeat(live, BLOCK)[:, None]
    projected = jnp.where(keep, frozen + adapted, 0.0).astype(jnp.bfloat16)
    return projected, grad_down, grad_up


def solution(mesh):
    rows = P(("group", "fsdp"), "tp")
    flat = P(("group", "fsdp"))
    in_specs = (rows, rows, P("fsdp", "tp"), rows, rows, flat, flat)
    return jax.shard_map(
        local, mesh=mesh, in_specs=in_specs, out_specs=(rows, rows, rows), check_vma=False
    )
```

time: 509 us -> 320 us (0.63)
  waiting for transfers between devices: 396 us -> 178 us
  blocking collectives: 38.7 us -> 76.5 us
  local copies, waits for them, and re-layouts: 11.3 us -> 4.09 us
  loops' own time: 6.54 us -> 0 us
    reduce_scatter x3 -> x0, waiting for transfers between devices: 223 us -> none  [the longest x1 152 us: local(): lax.psum_scatter(final_store[0], 'fsdp', scatter_dimension=0, tiled=True)]
    all_gather x1 -> x2, blocking collectives: 34.8 us -> 65.8 us  [gather(): return lax.all_gather(x, 'fsdp', axis=0, tiled=True)]
    unnamed x0 -> x1, blocking collectives: none -> 10.8 us
    broadcast_in_dim x4 -> x2, local copies, waits for them, and re-layouts: 8.86 us -> 0.1 us  [the longest x1 0.08 us: local(): keep = jnp.repeat(live, BLOCK)[:, None]]
    another operation x2 -> x0, loops' own time: 6.54 us -> none  [the longest x1 3.3 us: partial_stacks(): return lax.fori_loop(0, live_count, partial_loop_body, start)]
    all_gather x2 -> x3, waiting for transfers between devices: 171 us -> 177 us  [gather(): return lax.all_gather(x, 'fsdp', axis=0, tiled=True)]
    dot_general x12 -> x14, matrix products: 42.2 us -> 43 us  [the longest x2 20.2 us: frozen_half(): lax.dot_general(tokens, weight, CONTRACT, preferred_element_type=jnp.floa...]
  transfers between devices with their start and end apart: 5 -> 6, of which waited for: 5 -> 3; matrix products, arithmetic and copies ran while one was open for 0% -> 12% of each run, Pallas kernels for 0% -> 0%
where the time goes in v1:
time: 320 us
  waiting for transfers between devices  178 us (56%)
  blocking collectives  76.5 us (24%)
  matrix products  43 us (13%)
  between operations  16.5 us (5%)
  local copies, waits for them, and re-layouts  4.09 us (1%)
    all_gather x3, waiting for transfers between devices, gather(): return lax.all_gather(x, 'fsdp', axis=0, tiled=True)  177 us
    all_gather x2, blocking collectives, gather(): return lax.all_gather(x, 'fsdp', axis=0, tiled=True)  65.8 us
    dot_general x2, matrix products, frozen_half(): lax.dot_general(tokens, weight, CONTRACT, preferred_element_type=jnp.floa...  20.2 us
    unnamed x1, blocking collectives  10.8 us
    dot_general x2, matrix products, local(): lax.dot_general(back[s], x[s], COLUMNS, preferred_element_type=jnp.float32)  7.01 us
    dot_general x2, matrix products, local(): lax.dot_general(x[s], down[s], CONTRACT, preferred_element_type=jnp.float32)  6.97 us
  transfers between devices with their start and end apart: 6, of which 3 were waited for; matrix products, arithmetic and copies ran while one was open for 12% of the time, Pallas kernels for 0%

profile of v1, /device:TPU:0, one launch (start us, length us, event | category | flops | bytes accessed | tf_op | source)
XLA Modules:
  0.0 319.9 jit_solution(4546474300795171389)
XLA Ops:
  7.2 0.7 all-gather.6.cloned.1.call-update
  7.9 0.7 all-gather.4.cloned.1.call-update
  8.7 1.3 fusion.54
  11.3 34.8 %all_gather.20 = bf16[512,512]{1,0:T(8,128)(2,1)S(1)} all-gather(bf16[64,512]{1,0:T(8,128)(2,1)} %param.11), channel_id=1, replica_groups=mesh['group'=2,'fsdp'=8,'tp'=2] {'fsdp'}, dimensions={0}, use_global_device_ids=true | all-gather | bytes 589824 | tf_op jit(solution)/shard_map/all_gather | solution.py:16
  46.1 1.3 convolution_bitcast_fusion.1
  47.4 1.3 convolution_bitcast_fusion
  50.1 3.5 %fusion = bf16[16,4096]{1,0:T(8,128)(2,1)S(1)} fusion(bf16[1024,4096]{1,0:T(8,128)(2,1)} %param.7, f32[]{:T(128)} %bitcast.12, bf16[2,512,16]{1,2,0:T(8,128)(2,1)S(1)} %add_convert_fusion), kind=kOutput, calls=%fused_computation.2 | convolution fusion | flops 67239936 | bytes 4342272 | tf_op jit(solution)/shard_map/dot_general | solution.py:58
  53.6 3.5 %fusion.1 = bf16[16,4096]{1,0:T(8,128)(2,1)S(1)} fusion(bf16[1024,4096]{1,0:T(8,128)(2,1)} %param.7, f32[]{:T(128)} %bitcast.18, bf16[2,512,16]{1,2,0:T(8,128)(2,1)S(1)} %add_convert_fusion), kind=kOutput, calls=%fused_computation.3 | convolution fusion | flops 67239936 | bytes 4342272 | tf_op jit(solution)/shard_map/dot_general | solution.py:58
  57.1 0.7 pad_maximum_fusion
  57.9 0.7 dynamic-slice
  59.4 10.8 %all-reduce = s32[16]{0:T(128)S(1)} all-reduce(s32[16]{0:T(128)S(1)} %select_dynamic-update-slice_fusion), channel_id=1, replica_groups=mesh['group'=2,'fsdp'=8,'tp'=2] {'fsdp'}, use_global_device_ids=true, to_apply=%add | all-reduce | flops 16 | bytes 128
  70.4 19.1 %all-gather.6.cloned.1.call-done = bf16[512,4096]{1,0:T(8,128)(2,1)} async-done(((bf16[64,4096]{1,0:T(8,128)(2,1)}), bf16[512,4096]{1,0:T(8,128)(2,1)}) %all-gather.6.cloned.1.call-update) | async-done | bytes 4194320 | tf_op jit(solution)/shard_map/all_gather | solution.py:16
  89.6 3.4 %fusion.19 = f32[1,512,16]{1,2,0:T(8,128)S(1)} fusion(bf16[1024,4096]{1,0:T(8,128)(2,1)} %param.7, bf16[512,4096]{1,0:T(8,128)(2,1)} %all-gather.6.cloned.1.call-done, s32[]{:T(128)S(6)} %select_n.28), kind=kOutput, calls=%fused_computation.21 | convolution fusion | flops 67108864 | bytes 4358148 | tf_op jit(solution)/shard_map/dot_general | solution.py:68
  93.0 121.9 %all-gather.4.cloned.1.call-done = bf16[1024,4096]{1,0:T(8,128)(2,1)} async-done(((bf16[128,4096]{1,0:T(8,128)(2,1)}), bf16[1024,4096]{1,0:T(8,128)(2,1)}) %all-gather.4.cloned.1.call-update) | async-done | bytes 8388624 | tf_op jit(solution)/shard_map/all_gather | solution.py:16
  214.9 10.5 %fusion.16 = f32[1024,512]{0,1:T(8,128)} fusion(bf16[1024,4096]{1,0:T(8,128)(2,1)} %param.7, bf16[1024,4096]{1,0:T(8,128)(2,1)} %all-gather.4.cloned.1.call-done, s32[]{:T(128)S(6)} %select_n.27), kind=kOutput, calls=%fused_computation.18 | convolution fusion | flops 4294967296 | bytes 14680068 | tf_op jit(solution)/shard_map/dot_general | solution.py:86
  225.4 3.5 %fusion.22 = f32[1,512,16]{1,2,0:T(8,128)S(1)} fusion(bf16[1024,4096]{1,0:T(8,128)(2,1)} %param.7, bf16[512,4096]{1,0:T(8,128)(2,1)} %all-gather.6.cloned.1.call-done, s32[]{:T(128)S(6)} %select_n.29), kind=kOutput, calls=%fused_computation.22 | convolution fusion | flops 67108864 | bytes 4358148 | tf_op jit(solution)/shard_map/dot_general | solution.py:68
  229.5 35.6 %all-gather.8.cloned.1.call-done = bf16[256,4096]{1,0:T(8,128)(2,1)} async-done(((bf16[32,4096]{1,0:T(8,128)(2,1)}), bf16[256,4096]{1,0:T(8,128)(2,1)}) %all-gather.8.cloned.1.call-update) | async-done | bytes 2097168 | tf_op jit(solution)/shard_map/all_gather | solution.py:16
  265.1 3.1 fusion.35
  268.2 0.8 fusion.25
  269.0 0.8 fusion.26
  269.8 30.9 %all_gather.23 = bf16[256,512]{1,0:T(8,128)(2,1)S(1)} all-gather(bf16[32,512]{1,0:T(8,128)(2,1)S(1)} %pad_maximum_fusion.3), channel_id=1, replica_groups=mesh['group'=2,'fsdp'=8,'tp'=2] {'fsdp'}, dimensions={0}, use_global_device_ids=true | all-gather | bytes 294912 | tf_op jit(solution)/shard_map/all_gather | solution.py:16
  300.8 0.9 fusion.33
  302.3 9.7 %fusion.13 = bf16[1024,512]{0,1:T(8,128)(2,1)S(1)} fusion(f32[512,512]{0,1:T(8,128)S(1)} %convolution_multiply_fusion.2, f32[512,512]{0,1:T(8,128)S(1)} %convolution_multiply_fusion.3, f32[1024,512]{0,1:T(8,128)} %collective-permute-done, bf16[1024,4096]{1,0:T(8,128)(2,1)} %param.7, bf16[1024,4096]{1,0:T(8,128)(2,1)} %all-gather.4.cloned.1.call-done, ...), kind=kOutput, calls=%fused_computation.16 | convolution fusion | flops 4297588736 | bytes 17826820 | tf_op jit(solution)/shard_map/dot_general | solution.py:86
  312.0 1.3 copy.12
  (34 shorter events, 2.4 us)
Async XLA Ops:
  7.2 82.4 %all-gather.6.cloned.1.call-start = ((), (), s32[]{:S(2)}) async-start(), calls=%async_computation.1 | async-start | bytes 4718592 | tf_op jit(solution)/shard_map/all_gather | solution.py:16
  7.9 207.0 %all-gather.4.cloned.1.call-start = ((), (), s32[]{:S(2)}) async-start(), calls=%async_computation | async-start | bytes 9437184 | tf_op jit(solution)/shard_map/all_gather | solution.py:16
  8.6 256.4 %all-gather.8.cloned.1.call-start = ((), (), s32[]{:S(2)}) async-start(), calls=%async_computation.2 | async-start | bytes 2359296 | tf_op jit(solution)/shard_map/all_gather | solution.py:16
  48.7 1.3 collective-permute-start.2
  50.1 7.8 %copy-start.2 = (u32[32]{0:T(128)S(1)}, u32[32]{0:T(128)}, u32[]{:S(2)}) copy-start(u32[32]{0:T(128)} %constant.35) | copy-start | bytes 388
  50.1 9.2 %copy-start.1 = (s32[2]{0:T(128)S(1)}, s32[2]{0:T(128)}, u32[]{:S(2)}) copy-start(s32[2]{0:T(128)} %param.13) | copy-start | bytes 28
  225.4 42.8 %copy-start = (bf16[1024,512]{1,0:T(8,128)(2,1)S(1)}, bf16[1024,512]{1,0:T(8,128)(2,1)}, u32[]{:S(2)}) copy-start(bf16[1024,512]{1,0:T(8,128)(2,1)} %param.8) | copy-start | bytes 3145732
  225.4 76.9 %collective-permute-start = (f32[1024,512]{0,1:T(8,128)}, f32[1024,512]{0,1:T(8,128)}, u32[]{:S(2)}, u32[]{:S(2)}) collective-permute-start(f32[1024,512]{0,1:T(8,128)} %fusion.16), channel_id=1, source_target_pairs={{0,1},{1,0},{2,3},{3,2},{4,5},{5,4},{6,7},{7,6},{8,9},{9,8},{10,11... | collective-permute-start | bytes 6291464 | tf_op jit(solution)/shard_map/ppermute | solution.py:30
  229.0 39.2 %collective-permute-start.1 = (f32[2,512,16]{1,2,0:T(8,128)S(1)}, f32[2,512,16]{1,2,0:T(8,128)S(1)}, u32[]{:S(2)}, u32[]{:S(2)}) collective-permute-start(f32[2,512,16]{1,2,0:T(8,128)S(1)} %pad_maximum_fusion.1), channel_id=1, source_target_pairs={{0,1},{1,0},{2,3},{3,2},{4,5},{5,4},{6,7},{7,6},{8,9},{9,8},{10,11... | collective-permute-start | bytes 196616 | tf_op jit(solution)/shard_map/ppermute | solution.py:30
Sparse Core Ops, SparseCore 0:
  10.1 79.3 all-gather.5
  91.7 123.1 all-gather.3
  217.6 47.4 all-gather.7

commit v2 on v1

--- a/solution.py
+++ b/solution.py
@@ -1,6 +1,10 @@
+import functools
+
 import jax
 import jax.numpy as jnp
 from jax import lax
+from jax.experimental import pallas as pl
+from jax.experimental.pallas import tpu as pltpu
 from jax.sharding import PartitionSpec as P
 
 RANK = 16
@@ -12,8 +16,132 @@
 COLUMNS = (((0,), (0,)), ((), ()))
 
 
-def gather(x):
-    return lax.all_gather(x, "fsdp", axis=0, tiled=True)
+RING_LIMIT = 16
+MESH = pl.DeviceIdType.MESH
+
+
+def ring_kernel(n, plan, *refs):
+    count = len(plan)
+    ins, outs = refs[:count], refs[count : 2 * count]
+    own_sem, send_sem, recv_sem, x_send, x_recv = refs[2 * count :]
+    depth = n // 2
+    group, me, core = lax.axis_index("group"), lax.axis_index("fsdp"), lax.axis_index("tp")
+
+    def place(r):
+        far = r // depth
+        return 2 * (r + far * (2 * depth - 1 - 2 * r)) + far
+
+    row = me // 2
+    side = me % 2
+    spot = row + side * (2 * depth - 1 - 2 * row)
+    ways = (
+        (group, place((spot + 1) % n), core),
+        (group, place((spot + n - 1) % n), core),
+    )
+    across = (1 - group, me, core)
+    shares = any(shared for _, shared in plan)
+
+    barrier = pltpu.get_barrier_semaphore()
+    greeted = ways + ((across,) if shares else ())
+    for other in greeted:
+        pl.semaphore_signal(barrier, inc=1, device_id=other, device_id_type=MESH)
+    pl.semaphore_wait(barrier, len(greeted))
+
+    def pieces(k):
+        halves, shared = plan[k]
+        rows = ins[k].shape[0]
+        part = rows // 2 if shared else rows
+        size = part // halves
+        base = group * part if shared else 0
+        return [(base + h * size, size) for h in range(halves)]
+
+    copies, hand_overs = {}, []
+
+    def send(k, h, d, step):
+        low, size = pieces(k)[h]
+        origin = place((spot + (n - step if d == 0 else step)) % n)
+        there = pl.ds(pl.multiple_of(origin * ins[k].shape[0] + low, 8), size)
+        here = ins[k].at[pl.ds(pl.multiple_of(low, 8), size)] if step == 0 else outs[k].at[there]
+        at = k, h, d, step
+        copy = pltpu.make_async_remote_copy(
+            src_ref=here,
+            dst_ref=outs[k].at[there],
+            send_sem=send_sem.at[at],
+            recv_sem=recv_sem.at[at],
+            device_id=ways[d],
+            device_id_type=MESH,
+        )
+        copy.start()
+        copies[at] = copy
+
+    def arrived(k, h, d, step):
+        copies[k, h, d, step].wait_recv()
+        if plan[k][1]:
+            low, size = pieces(k)[h]
+            step = step + 1
+            origin = place((spot + (n - step if d == 0 else step)) % n)
+            there = outs[k].at[pl.ds(pl.multiple_of(origin * ins[k].shape[0] + low, 8), size)]
+            copy = pltpu.make_async_remote_copy(
+                src_ref=there,
+                dst_ref=there,
+                send_sem=x_send.at[h, d, step - 1],
+                recv_sem=x_recv.at[h, d, step - 1],
+                device_id=across,
+                device_id_type=MESH,
+            )
+            copy.start()
+            hand_overs.append(copy)
+
+    def hops(h, d):
+        return depth if h == d else depth - 1
+
+    own = []
+    for step in range(depth + 1):
+        for k in range(count):
+            for h in range(plan[k][0]):
+                for d in range(2):
+                    if 1 <= step <= hops(h, d):
+                        arrived(k, h, d, step - 1)
+                    if step < hops(h, d):
+                        send(k, h, d, step)
+        if step == 0:
+            for k in range(count):
+                rows = ins[k].shape[0]
+                copy = pltpu.make_async_copy(
+                    ins[k], outs[k].at[pl.ds(pl.multiple_of(me * rows, 8), rows)], own_sem.at[k]
+                )
+                copy.start()
+                own.append(copy)
+    for copy in hand_overs:
+        copy.wait_recv()
+    for copy in list(copies.values()) + hand_overs:
+        copy.wait_send()
+    for copy in own:
+        copy.wait()
+
+
+def gather(arrays, plan, identity):
+    n = lax.axis_size("fsdp")
+    if n > RING_LIMIT or n % 2 or lax.axis_size("group") != 2:
+        return [lax.all_gather(x, "fsdp", axis=0, tiled=True) for x in arrays]
+    sems = (len(arrays), 2, 2, n // 2)
+    whole = pl.BlockSpec(memory_space=pl.ANY)
+    moved = sum(x.size * x.dtype.itemsize for x in arrays)
+    return pl.pallas_call(
+        functools.partial(ring_kernel, n, plan),
+        out_shape=[jax.ShapeDtypeStruct((n * x.shape[0], x.shape[1]), x.dtype) for x in arrays],
+        in_specs=[whole] * len(arrays),
+        out_specs=[whole] * len(arrays),
+        scratch_shapes=[
+            pltpu.SemaphoreType.DMA((len(arrays),)),
+            pltpu.SemaphoreType.DMA(sems),
+            pltpu.SemaphoreType.DMA(sems),
+            pltpu.SemaphoreType.DMA(sems[1:]),
+            pltpu.SemaphoreType.DMA(sems[1:]),
+        ],
+        compiler_params=pltpu.CompilerParams(collective_id=identity, has_side_effects=True),
+        cost_estimate=pl.CostEstimate(flops=0, bytes_accessed=2 * n * moved, transcendentals=0),
+    )(*arrays)
 
 
 def rows_of(table, tenants):
@@ -42,8 +170,10 @@
     x = [tokens[s * BLOCK : (s + 1) * BLOCK] for s in range(SLOTS)]
     g = [cotangent[s * BLOCK : (s + 1) * BLOCK] for s in range(SLOTS)]
 
-    up_all = gather(rank_up)
-    ids_all = gather(jnp.where(live, tenants, -1))
+    ids = jnp.where(live, tenants, -1)
+    ids_tile = jnp.broadcast_to(jnp.pad(ids, (0, 8 - SLOTS))[:, None], (8, 128))
+    up_all, tiles_all = gather([rank_up, ids_tile], [(2, False), (1, False)], 0)
+    ids_all = tiles_all[:, 0].reshape(-1, 8)[:, :SLOTS].reshape(-1)
     mine = me * owned + jnp.arange(owned, dtype=jnp.int32)
     sent = (ids_all[:, None] * RANK + jnp.arange(RANK, dtype=jnp.int32)).reshape(-1)
     chosen = (mine[:, None] == sent[None, :]).astype(jnp.bfloat16)
@@ -59,9 +189,9 @@
             for s in range(SLOTS)
         ]
     ).astype(jnp.bfloat16)
-    down_all = gather(rank_down)
-    down_terms_all = gather(down_terms)
-    frozen_all = gather(frozen_rows)
+    frozen_all, down_all, down_terms_all = gather(
+        [frozen_rows, rank_down, down_terms], [(2, True), (2, False), (2, False)], 1
+    )
 
     down = rows_of(down_all, tenants)
     low_part = jnp.stack(
@@ -74,7 +204,7 @@
             for s in range(SLOTS)
         ]
     ).astype(jnp.bfloat16)
-    up_terms_all = gather(up_terms)
+    (up_terms_all,) = gather([up_terms], [(2, False)], 2)
     grad_down = owner_sum(down_terms_all, chosen)
     grad_up = owner_sum(up_terms_all, chosen)
 

time: 320 us -> 196 us (0.61)
  waiting for transfers between devices: 178 us -> 0.07 us
  Pallas kernels: 0 us -> 142 us
  blocking collectives: 76.5 us -> 0 us
  between operations: 16.5 us -> 2.78 us
    all_gather x3 -> x0, waiting for transfers between devices: 177 us -> none  [gather(): return lax.all_gather(x, 'fsdp', axis=0, tiled=True)]
    pallas_call x0 -> x3, Pallas kernels: none -> 142 us  [gather(): pl.pallas_call(functools.partial(ring_kernel, n, plan), out_shape=[jax.Sh...]
    all_gather x2 -> x0, blocking collectives: 65.8 us -> none  [gather(): return lax.all_gather(x, 'fsdp', axis=0, tiled=True)]
    unnamed x1 -> x0, blocking collectives: 10.8 us -> none
  transfers between devices with their start and end apart: 6 -> 3, of which waited for: 3 -> 1; matrix products, arithmetic and copies ran while one was open for 12% -> 6% of each run, Pallas kernels for 0% -> 8%
where the time goes in v2:
time: 196 us; the launch traced here: 195 us
  Pallas kernels  142 us (72%)
  matrix products  42.6 us (22%)
  local copies, waits for them, and re-layouts  5.11 us (3%)
  between operations  2.78 us (1%)
  other arithmetic  2.18 us (1%)
    pallas_call x3, Pallas kernels, gather(): pl.pallas_call(functools.partial(ring_kernel, n, plan), out_shape=[jax.Sh...  142 us
    dot_general x2, matrix products, frozen_half(): lax.dot_general(tokens, weight, CONTRACT, preferred_element_type=jnp.floa...  20.1 us
    dot_general x2, matrix products, local(): lax.dot_general(back[s], x[s], COLUMNS, preferred_element_type=jnp.float32)  6.99 us
    dot_general x2, matrix products, local(): lax.dot_general(x[s], down[s], CONTRACT, preferred_element_type=jnp.float32)  5.83 us
  transfers between devices with their start and end apart: 3, of which 1 were waited for; matrix products, arithmetic and copies ran while one was open for 6% of the time, Pallas kernels for 8%

profile of v2, /device:TPU:0, one launch (start us, length us, event | category | flops | bytes accessed | tf_op | source)
XLA Modules:
  0.0 195.2 jit_solution(729719934819340018)
XLA Ops:
  0.6 1.3 fusion.54
  3.9 0.7 broadcast_select_fusion
  4.6 0.7 broadcast_in_dim.43.refs_1_
  5.2 18.7 %shard_map.94 = (bf16[512,512]{1,0:T(8,128)(2,1)}, s32[64,128]{1,0:T(8,128)}) custom-call(bf16[64,512]{1,0:T(8,128)(2,1)} %refs_0_.2, s32[8,128]{1,0:T(8,128)} %broadcast_in_dim.43.refs_1_), custom_call_target="tpu_custom_call" | custom-call | bytes 1114112 | tf_op jit(solution)/shard_map/pallas_call | solution.py:130
  23.9 1.3 convolution_bitcast_fusion.1
  25.2 1.3 convolution_bitcast_fusion
  27.2 0.9 slice_reduce_fusion
  28.6 3.5 %fusion = bf16[16,4096]{1,0:T(8,128)(2,1)S(1)} fusion(bf16[1024,4096]{1,0:T(8,128)(2,1)} %param.7, f32[]{:T(128)} %bitcast.1, bf16[2,512,16]{1,2,0:T(8,128)(2,1)S(1)} %add_convert_fusion.1), kind=kOutput, calls=%fused_computation.2 | convolution fusion | flops 67239936 | bytes 4342272 | tf_op jit(solution)/shard_map/dot_general | solution.py:188
  32.1 3.5 %fusion.1 = bf16[16,4096]{1,0:T(8,128)(2,1)S(1)} fusion(bf16[1024,4096]{1,0:T(8,128)(2,1)} %param.7, f32[]{:T(128)} %bitcast.9, bf16[2,512,16]{1,2,0:T(8,128)(2,1)S(1)} %add_convert_fusion.1), kind=kOutput, calls=%fused_computation.3 | convolution fusion | flops 67239936 | bytes 4342272 | tf_op jit(solution)/shard_map/dot_general | solution.py:188
  35.6 0.7 pad_maximum_fusion.refs_2_
  36.3 108.5 %shard_map.95 = (bf16[1024,4096]{1,0:T(8,128)(2,1)}, bf16[512,4096]{1,0:T(8,128)(2,1)}, bf16[256,4096]{1,0:T(8,128)(2,1)}) custom-call(bf16[128,4096]{1,0:T(8,128)(2,1)} %refs_0_.3, bf16[64,4096]{1,0:T(8,128)(2,1)} %refs_1_.1, bf16[32,4096]{1,0:T(8,128)(2,1)} %pad_maximum_fusion.refs_2_), custom_call_target="tpu_custom_call" | custom-call | bytes 29360128 | tf_op jit(solution)/shard_map/pallas_call | solution.py:130
  144.8 3.6 %fusion.19 = f32[1,512,16]{1,2,0:T(8,128)S(1)} fusion(bf16[1024,4096]{1,0:T(8,128)(2,1)} %param.7, bf16[512,4096]{1,0:T(8,128)(2,1)} %get-tuple-element.10, s32[]{:T(128)S(6)} %select_n.28), kind=kOutput, calls=%fused_computation.21 | convolution fusion | flops 67108864 | bytes 4358148 | tf_op jit(solution)/shard_map/dot_general | solution.py:198
  148.4 10.7 %fusion.16 = f32[1024,512]{0,1:T(8,128)} fusion(bf16[1024,4096]{1,0:T(8,128)(2,1)} %param.7, bf16[1024,4096]{1,0:T(8,128)(2,1)} %get-tuple-element.9, s32[]{:T(128)S(6)} %select_n.31), kind=kOutput, calls=%fused_computation.18 | convolution fusion | flops 4294967296 | bytes 14680068 | tf_op jit(solution)/shard_map/dot_general | solution.py:216
  159.1 2.2 %fusion.22 = f32[1,512,16]{1,2,0:T(8,128)S(1)} fusion(bf16[1024,4096]{1,0:T(8,128)(2,1)S(1)} %bitcast.49, bf16[512,4096]{1,0:T(8,128)(2,1)} %get-tuple-element.10, s32[]{:T(128)S(6)} %select_n.29), kind=kOutput, calls=%fused_computation.22 | convolution fusion | flops 67108864 | bytes 4358148 | tf_op jit(solution)/shard_map/dot_general | solution.py:198
  161.7 1.5 fusion.35
  163.3 0.8 fusion.25
  164.1 0.8 fusion.26
  165.0 0.6 pad_maximum_fusion.3.refs_0_
  165.6 14.8 %shard_map.96 = bf16[256,512]{1,0:T(8,128)(2,1)} custom-call(bf16[32,512]{1,0:T(8,128)(2,1)} %pad_maximum_fusion.3.refs_0_), custom_call_target="tpu_custom_call" | custom-call | bytes 524288 | tf_op jit(solution)/shard_map/pallas_call | solution.py:130
  180.4 1.8 fusion.33
  182.3 1.1 convolution_multiply_fusion.3
  183.3 1.1 convolution_multiply_fusion.2
  184.4 9.4 %fusion.13 = bf16[1024,512]{0,1:T(8,128)(2,1)S(1)} fusion(f32[512,512]{0,1:T(8,128)S(1)} %convolution_multiply_fusion.2, f32[512,512]{0,1:T(8,128)S(1)} %convolution_multiply_fusion.3, f32[1024,512]{0,1:T(8,128)S(1)} %collective-permute-done.1, bf16[1024,4096]{1,0:T(8,128)(2,1)} %param.7, bf16[1024,4096]{1,0:T(8,128)(2,1)} %get-tuple-element.9, ...), kind=kOutput, calls=%fused_computation.16 | convolution fusion | flops 4297588736 | bytes 17826820 | tf_op jit(solution)/shard_map/dot_general | solution.py:216
  193.9 1.3 copy.15
  (31 shorter events, 1.6 us)
Async XLA Ops:
  26.5 2.0 %collective-permute-start = (f32[2,512,16]{1,2,0:T(8,128)S(1)}, f32[2,512,16]{1,2,0:T(8,128)S(1)}, u32[]{:S(2)}, u32[]{:S(2)}) collective-permute-start(f32[2,512,16]{1,2,0:T(8,128)S(1)} %pad_maximum_fusion.1), channel_id=1, source_target_pairs={{0,1},{1,0},{2,3},{3,2},{4,5},{5,4},{6,7},{7,6},{8,9},{9,8},{10,11... | collective-permute-start | bytes 196616 | tf_op jit(solution)/shard_map/ppermute | solution.py:158
  144.8 14.3 %slice-start = ((s8[8388608]{0:T(1024)(128)(4,1)}), s8[4194304]{0:T(1024)(128)(4,1)S(1)}, s32[]{:S(2)}) async-start(s8[8388608]{0:T(1024)(128)(4,1)} %bitcast.48), calls=%async_computation | async-start | bytes 8388608
  148.4 10.7 %slice-start.1 = ((s8[8388608]{0:T(1024)(128)(4,1)}), s8[4194304]{0:T(1024)(128)(4,1)S(1)}, s32[]{:S(2)}) async-start(s8[8388608]{0:T(1024)(128)(4,1)} %bitcast.48), calls=%async_computation.1 | async-start | bytes 8388608
  159.0 2.7 %copy-start.1 = (bf16[256,4096]{1,0:T(8,128)(2,1)S(1)}, bf16[256,4096]{1,0:T(8,128)(2,1)}, u32[]{:S(2)}) copy-start(bf16[256,4096]{1,0:T(8,128)(2,1)} %get-tuple-element.12) | copy-start | bytes 6291460
  159.0 4.3 %copy-start = (bf16[1024,512]{1,0:T(8,128)(2,1)S(1)}, bf16[1024,512]{1,0:T(8,128)(2,1)}, u32[]{:S(2)}) copy-start(bf16[1024,512]{1,0:T(8,128)(2,1)} %param.8) | copy-start | bytes 3145732
  159.0 25.4 %collective-permute-start.1 = (f32[1024,512]{0,1:T(8,128)}, f32[1024,512]{0,1:T(8,128)S(1)}, u32[]{:S(2)}, u32[]{:S(2)}) collective-permute-start(f32[1024,512]{0,1:T(8,128)} %fusion.16), channel_id=1, source_target_pairs={{0,1},{1,0},{2,3},{3,2},{4,5},{5,4},{6,7},{7,6},{8,9},{9,8},{10,11... | collective-permute-start | bytes 6291464 | tf_op jit(solution)/shard_map/ppermute | solution.py:158
  161.3 2.0 %collective-permute-start.2 = (f32[2,512,16]{1,2,0:T(8,128)S(1)}, f32[2,512,16]{1,2,0:T(8,128)S(1)}, u32[]{:S(2)}, u32[]{:S(2)}) collective-permute-start(f32[2,512,16]{1,2,0:T(8,128)S(1)} %pad_maximum_fusion.2), channel_id=1, source_target_pairs={{0,1},{1,0},{2,3},{3,2},{4,5},{5,4},{6,7},{7,6},{8,9},{9,8},{10,11... | collective-permute-start | bytes 196616 | tf_op jit(solution)/shard_map/ppermute | solution.py:158

commit v3 on v2

--- a/solution.py
+++ b/solution.py
@@ -17,13 +17,21 @@
 
 
 RING_LIMIT = 16
+TILE = 256
 MESH = pl.DeviceIdType.MESH
 
 
-def ring_kernel(n, plan, *refs):
+def ring_kernel(n, plan, fused, *refs):
     count = len(plan)
     ins, outs = refs[:count], refs[count : 2 * count]
-    own_sem, send_sem, recv_sem, x_send, x_recv = refs[2 * count :]
+    own_sem, send_sem, recv_sem, x_send, x_recv = refs[2 * count : 2 * count + 5]
+    if fused:
+        ins = refs[:count]
+        tokens_ref, product_ref = refs[count], refs[count + 1]
+        outs = refs[count + 2 : 2 * count + 1]
+        (own_sem, send_sem, recv_sem, x_send, x_recv, gathered, held, part, other_part,
+         load_sem, swap_send, swap_recv) = refs[2 * count + 1 :]
+        outs = (gathered,) + tuple(outs)
     depth = n // 2
     group, me, core = lax.axis_index("group"), lax.axis_index("fsdp"), lax.axis_index("tp")
 
@@ -39,10 +47,11 @@
         (group, place((spot + n - 1) % n), core),
     )
     across = (1 - group, me, core)
+    twin = (group, me, 1 - core)
     shares = any(shared for _, shared in plan)
 
     barrier = pltpu.get_barrier_semaphore()
-    greeted = ways + ((across,) if shares else ())
+    greeted = ways + ((across,) if shares else ()) + ((twin,) if fused else ())
     for other in greeted:
         pl.semaphore_signal(barrier, inc=1, device_id=other, device_id_type=MESH)
     pl.semaphore_wait(barrier, len(greeted))
@@ -90,13 +99,61 @@
                 device_id_type=MESH,
             )
             copy.start()
-            hand_overs.append(copy)
+            hand_overs.append((step - 1, copy))
 
     def hops(h, d):
         return depth if h == d else depth - 1
 
+    def swap(origin):
+        return pltpu.make_async_remote_copy(
+            src_ref=part.at[origin],
+            dst_ref=other_part.at[origin % depth],
+            send_sem=swap_send.at[origin % depth],
+            recv_sem=swap_recv.at[origin % depth],
+            device_id=twin,
+            device_id_type=MESH,
+        )
+
+    def multiply(away):
+        origin = place((spot + away + n) % n)
+        rows = ins[0].shape[0]
+        chunk = pl.ds(pl.multiple_of(origin * rows, 8), rows)
+
+        def tile(t, carried):
+            block = pl.ds(pl.multiple_of(t * TILE, TILE), TILE)
+            part[origin, block] = lax.dot_general(
+                held[block], gathered[chunk], CONTRACT, preferred_element_type=jnp.float32
+            )
+            return carried
+
+        lax.fori_loop(0, held.shape[0] // TILE, tile, 0)
+
+        @pl.when(origin // depth != core)
+        def _():
+            swap(origin).start()
+
+    def use(distance):
+        if not fused:
+            return
+        if distance == 0:
+            loaded.wait()
+            own[0].wait()
+            multiply(0)
+            return
+        for copy in [c for at, c in hand_overs if at == distance - 1]:
+            copy.wait_recv()
+        multiply(distance)
+        if distance < depth:
+            multiply(-distance)
+
     own = []
+    if fused:
+        loaded = pltpu.make_async_copy(tokens_ref, held, load_sem)
     for step in range(depth + 1):
+        if step >= 2:
+            use(step - 2)
+        if step == depth:
+            use(step - 1)
         for k in range(count):
             for h in range(plan[k][0]):
                 for d in range(2):
@@ -112,36 +169,84 @@
                 )
                 copy.start()
                 own.append(copy)
-    for copy in hand_overs:
-        copy.wait_recv()
-    for copy in list(copies.values()) + hand_overs:
+            if fused:
+                loaded.start()
+    if fused:
+        use(depth)
+        for j in range(depth):
+            swap((1 - core) * depth + j).wait()
+            rows = ins[0].shape[0]
+            product_ref[:, j * rows : (j + 1) * rows] = part[core * depth + j] + other_part[j]
+    else:
+        for _, copy in hand_overs:
+            copy.wait_recv()
+    for copy in list(copies.values()) + [c for _, c in hand_overs]:
         copy.wait_send()
-    for copy in own:
+    for copy in own[1:] if fused else own:
         copy.wait()
 
 
-def gather(arrays, plan, identity):
+def gather(arrays, plan, identity, tokens=None):
     n = lax.axis_size("fsdp")
+    fused = tokens is not None
     if n > RING_LIMIT or n % 2 or lax.axis_size("group") != 2:
-        return [lax.all_gather(x, "fsdp", axis=0, tiled=True) for x in arrays]
+        full = [lax.all_gather(x, "fsdp", axis=0, tiled=True) for x in arrays]
+        return [cores_product(tokens, full[0])] + full[1:] if fused else full
     sems = (len(arrays), 2, 2, n // 2)
     whole = pl.BlockSpec(memory_space=pl.ANY)
     moved = sum(x.size * x.dtype.itemsize for x in arrays)
+    out_shape = [jax.ShapeDtypeStruct((n * x.shape[0], x.shape[1]), x.dtype) for x in arrays]
+    out_specs = [whole] * len(arrays)
+    operands = list(arrays)
+    scratch = [
+        pltpu.SemaphoreType.DMA((len(arrays),)),
+        pltpu.SemaphoreType.DMA(sems),
+        pltpu.SemaphoreType.DMA(sems),
+        pltpu.SemaphoreType.DMA(sems[1:]),
+        pltpu.SemaphoreType.DMA(sems[1:]),
+    ]
+    flops = 0
+    limit = None
+    if fused:
+        tall, wide = tokens.shape
+        rows = arrays[0].shape[0]
+        operands.append(tokens)
+        scratch += [
+            pltpu.VMEM(out_shape[0].shape, arrays[0].dtype),
+            pltpu.VMEM((tall, wide), tokens.dtype),
+            pltpu.VMEM((n, tall, rows), jnp.float32),
+            pltpu.VMEM((n // 2, tall, rows), jnp.float32),
+            pltpu.SemaphoreType.DMA,
+            pltpu.SemaphoreType.DMA((n // 2,)),
+            pltpu.SemaphoreType.DMA((n // 2,)),
+        ]
+        out_shape[0] = jax.ShapeDtypeStruct((tall, n // 2 * rows), jnp.float32)
+        out_specs[0] = pl.BlockSpec(memory_space=pltpu.VMEM)
+        flops = 2 * tall * wide * n * rows
+        limit = 40 * 1024 * 1024
     return pl.pallas_call(
-        functools.partial(ring_kernel, n, plan),
-        out_shape=[jax.ShapeDtypeStruct((n * x.shape[0], x.shape[1]), x.dtype) for x in arrays],
-        in_specs=[whole] * len(arrays),
-        out_specs=[whole] * len(arrays),
-        scratch_shapes=[
-            pltpu.SemaphoreType.DMA((len(arrays),)),
-            pltpu.SemaphoreType.DMA(sems),
-            pltpu.SemaphoreType.DMA(sems),
-            pltpu.SemaphoreType.DMA(sems[1:]),
-            pltpu.SemaphoreType.DMA(sems[1:]),
-        ],
-        compiler_params=pltpu.CompilerParams(collective_id=identity, has_side_effects=True),
-        cost_estimate=pl.CostEstimate(flops=0, bytes_accessed=2 * n * moved, transcendentals=0),
-    )(*arrays)
+        functools.partial(ring_kernel, n, plan, fused),
+        out_shape=out_shape,
+        in_specs=[whole] * len(operands),
+        out_specs=out_specs,
+        scratch_shapes=scratch,
+        compiler_params=pltpu.CompilerParams(
+            collective_id=identity, has_side_effects=True, vmem_limit_bytes=limit
+        ),
+        cost_estimate=pl.CostEstimate(flops=flops, bytes_accessed=2 * n * moved, transcendentals=0),
+    )(*operands)
+
+
+def cores_product(tokens, frozen_all):
+    half = frozen_all.shape[0] // 2
+    core = lax.axis_index("tp")
+
+    def frozen_half(which):
+        weight = lax.dynamic_slice_in_dim(frozen_all, which * half, half, 0)
+        return lax.dot_general(tokens, weight, CONTRACT, preferred_element_type=jnp.float32)
+
+    received = swap_cores(frozen_half(1 - core))
+    return frozen_half(core) + received
 
 
 def rows_of(table, tenants):
@@ -172,7 +277,9 @@
 
     ids = jnp.where(live, tenants, -1)
     ids_tile = jnp.broadcast_to(jnp.pad(ids, (0, 8 - SLOTS))[:, None], (8, 128))
-    up_all, tiles_all = gather([rank_up, ids_tile], [(2, False), (1, False)], 0)
+    up_all, tiles_all, down_all = gather(
+        [rank_up, ids_tile, rank_down], [(2, False), (1, False), (2, False)], 0
+    )
     ids_all = tiles_all[:, 0].reshape(-1, 8)[:, :SLOTS].reshape(-1)
     mine = me * owned + jnp.arange(owned, dtype=jnp.int32)
     sent = (ids_all[:, None] * RANK + jnp.arange(RANK, dtype=jnp.int32)).reshape(-1)
@@ -189,10 +296,6 @@
             for s in range(SLOTS)
         ]
     ).astype(jnp.bfloat16)
-    frozen_all, down_all, down_terms_all = gather(
-        [frozen_rows, rank_down, down_terms], [(2, True), (2, False), (2, False)], 1
-    )
-
     down = rows_of(down_all, tenants)
     low_part = jnp.stack(
         [lax.dot_general(x[s], down[s], CONTRACT, preferred_element_type=jnp.float32) for s in range(SLOTS)]
@@ -204,19 +307,12 @@
             for s in range(SLOTS)
         ]
     ).astype(jnp.bfloat16)
-    (up_terms_all,) = gather([up_terms], [(2, False)], 2)
+    frozen, down_terms_all, up_terms_all = gather(
+        [frozen_rows, down_terms, up_terms], [(2, True), (2, False), (2, False)], 1, tokens
+    )
     grad_down = owner_sum(down_terms_all, chosen)
     grad_up = owner_sum(up_terms_all, chosen)
 
-    half = cotangent.shape[1]
-    core = lax.axis_index("tp")
-
-    def frozen_half(which):
-        weight = lax.dynamic_slice_in_dim(frozen_all, which * half, half, 0)
-        return lax.dot_general(tokens, weight, CONTRACT, preferred_element_type=jnp.float32)
-
-    received = swap_cores(frozen_half(1 - core))
-    frozen = frozen_half(core) + received
     adapted = jnp.concatenate(
         [
             SCALE * jnp.dot(low[s], up[s], preferred_element_type=jnp.float32)

time: 196 us -> 186 us (0.949)
  matrix products: 42.6 us -> 22.1 us
  Pallas kernels: 142 us -> 151 us
    dot_general x2 -> x0, matrix products: 20.1 us -> none  [frozen_half(): lax.dot_general(tokens, weight, CONTRACT, preferred_element_type=jnp.floa...]
    pallas_call x3 -> x2, Pallas kernels: 142 us -> 151 us  [gather(): pl.pallas_call(functools.partial(ring_kernel, n, plan, fused), out_shape=...]
    unnamed x9 -> x8, local copies, waits for them, and re-layouts: 1.34 us -> 3.39 us
  transfers between devices with their start and end apart: 3 -> 2, of which waited for: 1 -> 0; matrix products, arithmetic and copies ran while one was open for 6% -> 3% of each run, Pallas kernels for 8% -> 0%
where the time goes in v3:
time: 186 us; the launch traced here: 185 us
  Pallas kernels  151 us (81%)
  matrix products  22.1 us (12%)
  local copies, waits for them, and re-layouts  6.4 us (3%)
  between operations  2.75 us (1%)
  other arithmetic  2.07 us (1%)
    pallas_call x2, Pallas kernels, gather(): pl.pallas_call(functools.partial(ring_kernel, n, plan, fused), out_shape=...  151 us
    dot_general x2, matrix products, local(): lax.dot_general(back[s], x[s], COLUMNS, preferred_element_type=jnp.float32)  7.08 us
    dot_general x2, matrix products, local(): lax.dot_general(x[s], down[s], CONTRACT, preferred_element_type=jnp.float32)  6.99 us
  transfers between devices with their start and end apart: 2, of which 0 were waited for; matrix products, arithmetic and copies ran while one was open for 3% of the time, Pallas kernels for 0%

profile of v3, /device:TPU:0, one launch (start us, length us, event | category | flops | bytes accessed | tf_op | source)
XLA Modules:
  0.0 185.0 jit_solution(13830071335358172793)
XLA Ops:
  0.6 1.3 fusion.43
  3.9 0.7 broadcast_select_fusion
  4.6 0.7 broadcast_in_dim.43.refs_1_
  5.2 52.1 %shard_map.94 = (bf16[512,512]{1,0:T(8,128)(2,1)}, s32[64,128]{1,0:T(8,128)}, bf16[512,4096]{1,0:T(8,128)(2,1)}) custom-call(bf16[64,512]{1,0:T(8,128)(2,1)} %refs_0_.2, s32[8,128]{1,0:T(8,128)} %broadcast_in_dim.43.refs_1_, bf16[64,4096]{1,0:T(8,128)(2,1)} %refs_2_.1), custom_call_target="tpu_custom_call" | custom-call | bytes 9502720 | tf_op jit(solution)/shard_map/pallas_call | solution.py:227
  57.3 3.5 %fusion.10 = f32[1,512,16]{1,2,0:T(8,128)S(1)} fusion(bf16[1024,4096]{1,0:T(8,128)(2,1)} %refs_3_.1, bf16[512,4096]{1,0:T(8,128)(2,1)} %get-tuple-element.10, s32[]{:T(128)S(6)} %select_n.22), kind=kOutput, calls=%fused_computation.15 | convolution fusion | flops 67108864 | bytes 4358148 | tf_op jit(solution)/shard_map/dot_general | solution.py:301
  60.9 3.5 %fusion.13 = f32[1,512,16]{1,2,0:T(8,128)S(1)} fusion(bf16[1024,4096]{1,0:T(8,128)(2,1)} %refs_3_.1, bf16[512,4096]{1,0:T(8,128)(2,1)} %get-tuple-element.10, s32[]{:T(128)S(6)} %select_n.23), kind=kOutput, calls=%fused_computation.16 | convolution fusion | flops 67108864 | bytes 4358148 | tf_op jit(solution)/shard_map/dot_general | solution.py:301
  64.4 1.0 convolution_bitcast_fusion.1
  65.4 1.0 convolution_bitcast_fusion
  66.4 0.5 collective-permute-start
  66.9 0.6 fusion.42
  67.5 0.1 slice_reduce_fusion
  67.7 0.1 mul.74
  67.9 0.1 add.59
  68.1 0.8 fusion.16
  68.9 0.8 fusion.17
  69.8 3.5 %fusion = bf16[16,4096]{1,0:T(8,128)(2,1)S(1)} fusion(bf16[1024,4096]{1,0:T(8,128)(2,1)} %refs_3_.1, f32[]{:T(128)} %bitcast.1, bf16[2,512,16]{1,2,0:T(8,128)(2,1)S(1)} %add_convert_fusion.1), kind=kOutput, calls=%fused_computation.2 | convolution fusion | flops 67239936 | bytes 4342272 | tf_op jit(solution)/shard_map/dot_general | solution.py:295
  73.3 3.6 %fusion.1 = bf16[16,4096]{1,0:T(8,128)(2,1)S(1)} fusion(bf16[1024,4096]{1,0:T(8,128)(2,1)} %refs_3_.1, f32[]{:T(128)} %bitcast.9, bf16[2,512,16]{1,2,0:T(8,128)(2,1)S(1)} %add_convert_fusion.1), kind=kOutput, calls=%fused_computation.3 | convolution fusion | flops 67239936 | bytes 4342272 | tf_op jit(solution)/shard_map/dot_general | solution.py:295
  76.9 1.0 convolution_multiply_fusion.3
  77.9 1.0 convolution_multiply_fusion.2
  79.0 3.4 %copy-done = bf16[1024,4096]{1,0:T(8,128)(2,1)S(1)} copy-done((bf16[1024,4096]{1,0:T(8,128)(2,1)S(1)}, bf16[1024,4096]{1,0:T(8,128)(2,1)}, u32[]{:S(2)}) %copy-start) | copy-done | bytes 8388632
  82.4 99.0 %shard_map.95 = (f32[1024,512]{1,0:T(8,128)S(1)}, bf16[256,4096]{1,0:T(8,128)(2,1)S(1)}, bf16[256,512]{1,0:T(8,128)(2,1)S(1)}) custom-call(bf16[128,4096]{1,0:T(8,128)(2,1)S(1)} %copy-done.1, bf16[32,4096]{1,0:T(8,128)(2,1)S(1)} %pad_maximum_fusion.refs_1_, bf16[32,512]{1,0:T(8,128)(2,1)S(1)} %pad_maximum_fusion.3.refs_2_, bf16[1024,4096]{1,0:T(8,128)(2,1)S(1)} %copy-done), custom_call_target="tpu_custom_call" | custom-call | flops 8589934592 | bytes 21495808 | tf_op jit(solution)/shard_map/pallas_call | solution.py:227
  181.4 0.9 fusion.24
  182.3 1.5 fusion.26
  183.8 1.2 fusion.9
  (25 shorter events, 0.5 us)
Async XLA Ops:
  57.3 7.1 %copy-start.2 = (bf16[1024,512]{1,0:T(8,128)(2,1)S(1)}, bf16[1024,512]{1,0:T(8,128)(2,1)}, u32[]{:S(2)}) copy-start(bf16[1024,512]{1,0:T(8,128)(2,1)} %param.8) | copy-start | bytes 3145732
  57.3 10.2 %copy-start.3 = (s32[64,128]{1,0:T(8,128)S(1)}, s32[64,128]{1,0:T(8,128)}, u32[]{:S(2)}) copy-start(s32[64,128]{1,0:T(8,128)} %get-tuple-element.12) | copy-start | bytes 98308
  64.4 3.7 %collective-permute-start.1 = (f32[2,512,16]{1,2,0:T(8,128)S(1)}, f32[2,512,16]{1,2,0:T(8,128)S(1)}, u32[]{:S(2)}, u32[]{:S(2)}) collective-permute-start(f32[2,512,16]{1,2,0:T(8,128)S(1)} %pad_maximum_fusion.2), channel_id=1, source_target_pairs={{0,1},{1,0},{2,3},{3,2},{4,5},{5,4},{6,7},{7,6},{8,9},{9,8},{10,11... | collective-permute-start | bytes 196616 | tf_op jit(solution)/shard_map/ppermute | solution.py:263
  66.4 3.4 %collective-permute-start = (f32[2,512,16]{1,2,0:T(8,128)S(1)}, f32[2,512,16]{1,2,0:T(8,128)S(1)}, u32[]{:S(2)}, u32[]{:S(2)}) collective-permute-start(f32[2,512,16]{1,2,0:T(8,128)S(1)} %pad_maximum_fusion.1), channel_id=1, source_target_pairs={{0,1},{1,0},{2,3},{3,2},{4,5},{5,4},{6,7},{7,6},{8,9},{9,8},{10,11... | collective-permute-start | bytes 196616 | tf_op jit(solution)/shard_map/ppermute | solution.py:263
  73.3 5.7 %copy-start.1 = (bf16[128,4096]{1,0:T(8,128)(2,1)S(1)}, bf16[128,4096]{1,0:T(8,128)(2,1)}, u32[]{:S(2)}) copy-start(bf16[128,4096]{1,0:T(8,128)(2,1)} %refs_0_.3) | copy-start | bytes 3145732
  79.0 3.4 %copy-start = (bf16[1024,4096]{1,0:T(8,128)(2,1)S(1)}, bf16[1024,4096]{1,0:T(8,128)(2,1)}, u32[]{:S(2)}) copy-start(bf16[1024,4096]{1,0:T(8,128)(2,1)} %refs_3_.1) | copy-start | bytes 25165828

commit v4 on v3

--- a/solution.py
+++ b/solution.py
@@ -17,7 +17,7 @@
 
 
 RING_LIMIT = 16
-TILE = 256
+TILE = 512
 MESH = pl.DeviceIdType.MESH
 
 
@@ -27,10 +27,10 @@
     own_sem, send_sem, recv_sem, x_send, x_recv = refs[2 * count : 2 * count + 5]
     if fused:
         ins = refs[:count]
-        tokens_ref, product_ref = refs[count], refs[count + 1]
-        outs = refs[count + 2 : 2 * count + 1]
+        tokens_ref, early_ref, product_ref = refs[count : count + 3]
+        outs = refs[count + 3 : 2 * count + 2]
         (own_sem, send_sem, recv_sem, x_send, x_recv, gathered, held, part, other_part,
-         load_sem, swap_send, swap_recv) = refs[2 * count + 1 :]
+         early, load_sem, swap_send, swap_recv) = refs[2 * count + 2 :]
         outs = (gathered,) + tuple(outs)
     depth = n // 2
     group, me, core = lax.axis_index("group"), lax.axis_index("fsdp"), lax.axis_index("tp")
@@ -114,41 +114,55 @@
             device_id_type=MESH,
         )
 
-    def multiply(away):
-        origin = place((spot + away + n) % n)
-        rows = ins[0].shape[0]
-        chunk = pl.ds(pl.multiple_of(origin * rows, 8), rows)
+    def multiply(*aways):
+        origins = [place((spot + away + n) % n) for away in aways]
+        late = ins[0].shape[0]
+        first = early.shape[0] // n
+        rows = first + late
 
         def tile(t, carried):
             block = pl.ds(pl.multiple_of(t * TILE, TILE), TILE)
-            part[origin, block] = lax.dot_general(
-                held[block], gathered[chunk], CONTRACT, preferred_element_type=jnp.float32
+            weight = jnp.concatenate(
+                [
+                    source[pl.ds(pl.multiple_of(origin * size, 8), size)]
+                    for origin in origins
+                    for source, size in ((early, first), (gathered, late))
+                ]
             )
+            product = lax.dot_general(
+                held[block], weight, CONTRACT, preferred_element_type=jnp.float32
+            )
+            for i, origin in enumerate(origins):
+                part[origin, block] = product[:, i * rows : (i + 1) * rows]
             return carried
 
         lax.fori_loop(0, held.shape[0] // TILE, tile, 0)
 
-        @pl.when(origin // depth != core)
-        def _():
-            swap(origin).start()
+        for origin in origins:
+
+            @pl.when(origin // depth != core)
+            def _(origin=origin):
+                swap(origin).start()
 
     def use(distance):
         if not fused:
             return
         if distance == 0:
-            loaded.wait()
+            for copy in loaded:
+                copy.wait()
             own[0].wait()
             multiply(0)
             return
         for copy in [c for at, c in hand_overs if at == distance - 1]:
             copy.wait_recv()
-        multiply(distance)
-        if distance < depth:
-            multiply(-distance)
+        multiply(*((distance, -distance) if distance < depth else (distance,)))
 
     own = []
     if fused:
-        loaded = pltpu.make_async_copy(tokens_ref, held, load_sem)
+        loaded = [
+            pltpu.make_async_copy(tokens_ref, held, load_sem.at[0]),
+            pltpu.make_async_copy(early_ref, early, load_sem.at[1]),
+        ]
     for step in range(depth + 1):
         if step >= 2:
             use(step - 2)
@@ -170,12 +184,13 @@
                 copy.start()
                 own.append(copy)
             if fused:
-                loaded.start()
+                for copy in loaded:
+                    copy.start()
     if fused:
         use(depth)
         for j in range(depth):
             swap((1 - core) * depth + j).wait()
-            rows = ins[0].shape[0]
+            rows = part.shape[2]
             product_ref[:, j * rows : (j + 1) * rows] = part[core * depth + j] + other_part[j]
     else:
         for _, copy in hand_overs:
@@ -186,12 +201,16 @@
         copy.wait()
 
 
-def gather(arrays, plan, identity, tokens=None):
+def gather(arrays, plan, identity, tokens=None, early=None):
     n = lax.axis_size("fsdp")
     fused = tokens is not None
     if n > RING_LIMIT or n % 2 or lax.axis_size("group") != 2:
         full = [lax.all_gather(x, "fsdp", axis=0, tiled=True) for x in arrays]
-        return [cores_product(tokens, full[0])] + full[1:] if fused else full
+        if fused:
+            both = [x.reshape(n, -1, x.shape[1]) for x in (early, full[0])]
+            joined = jnp.concatenate(both, axis=1).reshape(-1, early.shape[1])
+            full[0] = cores_product(tokens, joined)
+        return full
     sems = (len(arrays), 2, 2, n // 2)
     whole = pl.BlockSpec(memory_space=pl.ANY)
     moved = sum(x.size * x.dtype.itemsize for x in arrays)
@@ -209,14 +228,15 @@
     limit = None
     if fused:
         tall, wide = tokens.shape
-        rows = arrays[0].shape[0]
-        operands.append(tokens)
+        rows = arrays[0].shape[0] + early.shape[0] // n
+        operands += [tokens, early]
         scratch += [
             pltpu.VMEM(out_shape[0].shape, arrays[0].dtype),
             pltpu.VMEM((tall, wide), tokens.dtype),
             pltpu.VMEM((n, tall, rows), jnp.float32),
             pltpu.VMEM((n // 2, tall, rows), jnp.float32),
-            pltpu.SemaphoreType.DMA,
+            pltpu.VMEM(early.shape, early.dtype),
+            pltpu.SemaphoreType.DMA((2,)),
             pltpu.SemaphoreType.DMA((n // 2,)),
             pltpu.SemaphoreType.DMA((n // 2,)),
         ]
@@ -277,8 +297,11 @@
 
     ids = jnp.where(live, tenants, -1)
     ids_tile = jnp.broadcast_to(jnp.pad(ids, (0, 8 - SLOTS))[:, None], (8, 128))
-    up_all, tiles_all, down_all = gather(
-        [rank_up, ids_tile, rank_down], [(2, False), (1, False), (2, False)], 0
+    middle = frozen_rows.shape[0] // 2
+    up_all, tiles_all, down_all, early = gather(
+        [rank_up, ids_tile, rank_down, frozen_rows[:middle]],
+        [(2, False), (1, False), (2, False), (2, True)],
+        0,
     )
     ids_all = tiles_all[:, 0].reshape(-1, 8)[:, :SLOTS].reshape(-1)
     mine = me * owned + jnp.arange(owned, dtype=jnp.int32)
@@ -308,7 +331,11 @@
         ]
     ).astype(jnp.bfloat16)
     frozen, down_terms_all, up_terms_all = gather(
-        [frozen_rows, down_terms, up_terms], [(2, True), (2, False), (2, False)], 1, tokens
+        [frozen_rows[middle:], down_terms, up_terms],
+        [(2, True), (2, False), (2, False)],
+        1,
+        tokens,
+        early,
     )
     grad_down = owner_sum(down_terms_all, chosen)
     grad_up = owner_sum(up_terms_all, chosen)

time: 186 us -> 168 us (0.903)
  Pallas kernels: 151 us -> 135 us
    pallas_call x2, Pallas kernels: 151 us -> 135 us  [gather(): pl.pallas_call(functools.partial(ring_kernel, n, plan, fused), out_shape=...]
    unnamed x8 -> x6, local copies, waits for them, and re-layouts: 3.39 us -> 0.01 us
    slice x0 -> x1, local copies, waits for them, and re-layouts: none -> 2.08 us  [local(): frozen_rows[:middle]]
where the time goes in v4:
time: 168 us
  Pallas kernels  135 us (80%)
  matrix products  22.3 us (13%)
  local copies, waits for them, and re-layouts  5.1 us (3%)
  between operations  2.74 us (2%)
  other arithmetic  2.07 us (1%)
    pallas_call x2, Pallas kernels, gather(): pl.pallas_call(functools.partial(ring_kernel, n, plan, fused), out_shape=...  135 us
    dot_general x2, matrix products, local(): lax.dot_general(back[s], x[s], COLUMNS, preferred_element_type=jnp.float32)  7.3 us
    dot_general x2, matrix products, local(): lax.dot_general(x[s], down[s], CONTRACT, preferred_element_type=jnp.float32)  6.99 us
  transfers between devices with their start and end apart: 2, of which 0 were waited for; matrix products, arithmetic and copies ran while one was open for 3% of the time, Pallas kernels for 0%

profile of v4, /device:TPU:0, one launch (start us, length us, event | category | flops | bytes accessed | tf_op | source)
XLA Modules:
  0.0 167.7 jit_solution(16802984897623997918)
XLA Ops:
  0.6 1.3 fusion.44
  3.9 0.7 broadcast_select_fusion
  4.6 2.1 %fusion.42 = (bf16[64,4096]{1,0:T(8,128)(2,1)}, bf16[64,4096]{1,0:T(8,128)(2,1)S(1)}) fusion(bf16[128,4096]{1,0:T(8,128)(2,1)} %param.9), kind=kLoop, calls=%fused_computation.64 | loop fusion | bytes 2097152 | tf_op jit(solution)/shard_map/slice | solution.py:302
  6.6 0.7 broadcast_in_dim.43.refs_1_
  7.3 78.3 %shard_map.94 = (bf16[512,512]{1,0:T(8,128)(2,1)}, s32[64,128]{1,0:T(8,128)}, bf16[512,4096]{1,0:T(8,128)(2,1)}, bf16[512,4096]{1,0:T(8,128)(2,1)}) custom-call(bf16[64,512]{1,0:T(8,128)(2,1)} %refs_0_.1, s32[8,128]{1,0:T(8,128)} %broadcast_in_dim.43.refs_1_, bf16[64,4096]{1,0:T(8,128)(2,1)} %refs_2_.1, bf16[64,4096]{1,0:T(8,128)(2,1)} %get-tuple-element.17.refs_3_), custom_call_target="tpu_custom_call" | custom-call | bytes 17891328 | tf_op jit(solution)/shard_map/pallas_call | solution.py:247
  85.7 3.5 %fusion.13 = f32[1,512,16]{1,2,0:T(8,128)S(1)} fusion(bf16[1024,4096]{1,0:T(8,128)(2,1)} %refs_3_.1, bf16[512,4096]{1,0:T(8,128)(2,1)} %get-tuple-element.11, s32[]{:T(128)S(6)} %select_n.23), kind=kOutput, calls=%fused_computation.16 | convolution fusion | flops 67108864 | bytes 4358148 | tf_op jit(solution)/shard_map/dot_general | solution.py:324
  89.2 3.5 %fusion.10 = f32[1,512,16]{1,2,0:T(8,128)S(1)} fusion(bf16[1024,4096]{1,0:T(8,128)(2,1)} %refs_3_.1, bf16[512,4096]{1,0:T(8,128)(2,1)} %get-tuple-element.11, s32[]{:T(128)S(6)} %select_n.22), kind=kOutput, calls=%fused_computation.15 | convolution fusion | flops 67108864 | bytes 4358148 | tf_op jit(solution)/shard_map/dot_general | solution.py:324
  92.8 1.0 convolution_bitcast_fusion
  93.7 1.0 convolution_bitcast_fusion.1
  94.7 0.5 collective-permute-start
  95.3 0.6 fusion.43
  95.9 0.1 slice_reduce_fusion
  96.1 0.1 mul.74
  96.3 0.1 add.59
  96.4 0.8 fusion.17
  97.2 0.8 fusion.16
  98.1 3.5 %fusion.1 = bf16[16,4096]{1,0:T(8,128)(2,1)S(1)} fusion(bf16[1024,4096]{1,0:T(8,128)(2,1)} %refs_3_.1, f32[]{:T(128)} %bitcast.9, bf16[2,512,16]{1,2,0:T(8,128)(2,1)S(1)} %add_convert_fusion.1), kind=kOutput, calls=%fused_computation.3 | convolution fusion | flops 67239936 | bytes 4342272 | tf_op jit(solution)/shard_map/dot_general | solution.py:318
  101.6 3.8 %fusion = bf16[16,4096]{1,0:T(8,128)(2,1)S(1)} fusion(bf16[1024,4096]{1,0:T(8,128)(2,1)} %refs_3_.1, f32[]{:T(128)} %bitcast.1, bf16[2,512,16]{1,2,0:T(8,128)(2,1)S(1)} %add_convert_fusion.1), kind=kOutput, calls=%fused_computation.2 | convolution fusion | flops 67239936 | bytes 4342272 | tf_op jit(solution)/shard_map/dot_general | solution.py:318
  105.4 1.0 convolution_multiply_fusion.2
  106.5 1.0 convolution_multiply_fusion.3
  107.6 56.6 %shard_map.95 = (f32[1024,512]{1,0:T(8,128)S(1)}, bf16[256,4096]{1,0:T(8,128)(2,1)S(1)}, bf16[256,512]{1,0:T(8,128)(2,1)S(1)}) custom-call(bf16[64,4096]{1,0:T(8,128)(2,1)S(1)} %get-tuple-element.18.refs_0_, bf16[32,4096]{1,0:T(8,128)(2,1)S(1)} %pad_maximum_fusion.refs_1_, bf16[32,512]{1,0:T(8,128)(2,1)S(1)} %pad_maximum_fusion.3.refs_2_, ...), custom_call_target="tpu_custom_call" | custom-call | flops 8589934592 | bytes 13107200 | tf_op jit(solution)/shard_map/pallas_call | solution.py:247
  164.1 0.9 fusion.24
  165.0 1.5 fusion.26
  166.5 1.2 fusion.9
  (24 shorter events, 0.5 us)
Async XLA Ops:
  85.6 7.1 %copy-start.1 = (bf16[1024,512]{1,0:T(8,128)(2,1)S(1)}, bf16[1024,512]{1,0:T(8,128)(2,1)}, u32[]{:S(2)}) copy-start(bf16[1024,512]{1,0:T(8,128)(2,1)} %param.8) | copy-start | bytes 3145732
  85.6 10.3 %copy-start.2 = (s32[64,128]{1,0:T(8,128)S(1)}, s32[64,128]{1,0:T(8,128)}, u32[]{:S(2)}) copy-start(s32[64,128]{1,0:T(8,128)} %get-tuple-element.14) | copy-start | bytes 98308
  92.7 3.7 %collective-permute-start.1 = (f32[2,512,16]{1,2,0:T(8,128)S(1)}, f32[2,512,16]{1,2,0:T(8,128)S(1)}, u32[]{:S(2)}, u32[]{:S(2)}) collective-permute-start(f32[2,512,16]{1,2,0:T(8,128)S(1)} %pad_maximum_fusion.2), channel_id=1, source_target_pairs={{0,1},{1,0},{2,3},{3,2},{4,5},{5,4},{6,7},{7,6},{8,9},{9,8},{10,11... | collective-permute-start | bytes 196616 | tf_op jit(solution)/shard_map/ppermute | solution.py:283
  94.7 3.4 %collective-permute-start = (f32[2,512,16]{1,2,0:T(8,128)S(1)}, f32[2,512,16]{1,2,0:T(8,128)S(1)}, u32[]{:S(2)}, u32[]{:S(2)}) collective-permute-start(f32[2,512,16]{1,2,0:T(8,128)S(1)} %pad_maximum_fusion.1), channel_id=1, source_target_pairs={{0,1},{1,0},{2,3},{3,2},{4,5},{5,4},{6,7},{7,6},{8,9},{9,8},{10,11... | collective-permute-start | bytes 196616 | tf_op jit(solution)/shard_map/ppermute | solution.py:283
  101.6 5.9 %copy-start = (bf16[512,4096]{1,0:T(8,128)(2,1)S(1)}, bf16[512,4096]{1,0:T(8,128)(2,1)}, u32[]{:S(2)}) copy-start(bf16[512,4096]{1,0:T(8,128)(2,1)} %get-tuple-element.12.refs_4_) | copy-start | bytes 12582916
